TPU v7x, 32 devices: a whole 2x2x4 slice. The times are simulated.
32 devices in a mesh: group: 2 (over y), space: 8 (over z, x), tm: 2 (over core).
Axes of the slice: x: 2, y: 2, z: 4, core: 2. Of those that a mesh axis runs over, the one named last changes fastest.
Arguments:
- w_modes: bfloat16 [12, 1024, 768], P(('group', 'tm'), 'space'), parts along dimension 0, may hold values from -6 to 6
- v_modes: bfloat16 [12, 1024, 768], P(('group', 'tm'), 'space'), parts along dimension 0, may hold values from -6 to 6
- phase_index: int32 [1024], P('space'), may hold values from 0 to 95
- seq_offset: int32 [6], replicated, may hold values from 1 to 5
- owner_block: int32 [8], replicated, may hold values from 0 to 7, each once
Outputs:
- strips: float32 [384, 12, 768], P('space', ('group', 'tm')), parts along dimension 1
- margin: float32 [12, 768], P(('group', 'tm')), parts along dimension 0
There are 2 independent parts, one for each index of `group`. A program takes and returns all parts, laid end to end along the dimension named above; an argument that names none is the same for every part. Nothing has to cross between parts.
Inputs may be any that keep to these rules, and one draw needn't show every extreme that they name: owner_block is a permutation of 0 to 7.
All inputs are finite; a program needn't handle non-finite values.
Results may differ from a plain program's by a relative error of at most 0.0041.
Values may be sent and summed in bfloat16 or wider, within the bound.
A program may use at most 64 MiB of HBM per device.

v0:
```python
import math

import jax
import jax.numpy as jnp
from jax import lax
from jax.sharding import PartitionSpec as P

PHASES = 96


def from_behind(block, axis, distance):
    devices = range(lax.axis_size(axis))
    route = [((i - distance) % len(devices), i) for i in devices]
    return lax.ppermute(block, axis, route)


def shards(w_modes, v_modes, phase_index, seq_offset, owner_block):
    tdev, sdev, width = w_modes.shape
    nmode = width // 2
    nspace = lax.axis_size("space")
    ntm = lax.axis_size("tm")
    block = nmode // nspace
    total_slices = tdev * ntm
    scale_sites = 1.0 / math.sqrt(sdev * nspace)
    scale_modes = 1.0 / math.sqrt(2 * nmode)
    order = (owner_block[:, None] * block + jnp.arange(block, dtype=jnp.int32)[None, :]).reshape(-1)
    w_real = jnp.take(w_modes[:, :, :nmode], order, axis=2)
    w_imag = jnp.take(w_modes[:, :, nmode:], order, axis=2)
    left = jnp.concatenate([w_real, w_imag], axis=1)
    angle = phase_index.astype(jnp.float32) * (2.0 * math.pi / PHASES)
    cosv = jnp.cos(angle)[None, :, None]
    sinv = jnp.sin(angle)[None, :, None]
    v_real = v_modes[:, :, :nmode].astype(jnp.float32)
    v_imag = v_modes[:, :, nmode:].astype(jnp.float32)
    ph_real = (cosv * v_real + sinv * v_imag).astype(jnp.bfloat16)
    ph_imag = (cosv * v_imag - sinv * v_real).astype(jnp.bfloat16)
    right = jnp.concatenate(
        [jnp.concatenate([ph_real, ph_imag], axis=2), jnp.concatenate([ph_imag, -ph_real], axis=2)],
        axis=1,
    )
    rank = lax.axis_index("tm")
    global_slice = rank * tdev + jnp.arange(tdev, dtype=jnp.int32)
    target = (global_slice + jnp.take(seq_offset, global_slice)) % total_slices
    pick = (target - rank * tdev) % total_slices
    v_two = jnp.concatenate(
        [
            jnp.concatenate([v_modes[:, :, :nmode], -v_modes[:, :, nmode:]], axis=2),
            jnp.concatenate([v_modes[:, :, nmode:], v_modes[:, :, :nmode]], axis=2),
        ],
        axis=1,
    )
    full = lax.psum(
        jnp.einsum("tsi,tsj->itj", left, right, preferred_element_type=jnp.float32) * scale_sites,
        "space",
    )
    strips = lax.dynamic_slice_in_dim(full, lax.axis_index("space") * block, block, 0)
    rounded = full.astype(jnp.bfloat16)
    pieces = [rounded]
    pieces.append(from_behind(rounded, "tm", -1))
    chosen = jnp.take(jnp.concatenate(pieces, axis=1), pick, axis=1)
    seq_raw = jnp.einsum("tsj,itj->tsi", v_two, chosen, preferred_element_type=jnp.float32)
    seq = seq_raw * scale_modes
    seq_real = seq[:, :sdev]
    seq_imag = seq[:, sdev:]
    wr_full = w_real.astype(jnp.float32)
    wi_full = w_imag.astype(jnp.float32)
    over_real = jnp.sum(wr_full * seq_real + wi_full * seq_imag, axis=1) * scale_sites
    over_imag = jnp.sum(wr_full * seq_imag - wi_full * seq_real, axis=1) * scale_sites
    total_real, total_imag = lax.psum((over_real, over_imag), "space")
    margin = jnp.zeros((tdev, 2 * nmode), jnp.float32)
    margin = margin.at[:, order].set(total_real).at[:, order + nmode].set(total_imag)
    return (strips, margin)


def solution(mesh):
    in_specs = (
        P(("group", "tm"), "space", None),
        P(("group", "tm"), "space", None),
        P("space"),
        P(),
        P(),
    )
    out_specs = (P("space", ("group", "tm"), None), P(("group", "tm"), None))
    return jax.shard_map(shards, mesh=mesh, in_specs=in_specs, out_specs=out_specs, check_vma=False)
```

profile of v0, /device:TPU:0, one launch (start us, length us, event | category | flops | bytes accessed | tf_op | source)
XLA Modules:
  0.0 221.3 jit_solution(14172420527783329290)
XLA Ops:
  7.2 1.1 fusion.53
  8.9 0.9 fusion.50
  10.2 0.3 copy.39
  10.5 2.0 gather_fusion.2
  12.5 0.3 copy.26
  12.8 0.3 copy.40
  13.1 2.0 gather_fusion.3
  15.1 0.3 copy.28
  15.5 0.7 copy-done.4
  16.3 2.6 %multiply_bitcast_fusion = f32[384,3,768]{0,2,1:T(8,128)} fusion(bf16[3,128,384]{1,2,0:T(8,128)(2,1)S(1)} %get-tuple-element.15, bf16[3,128,384]{1,2,0:T(8,128)(2,1)S(1)} %fusion.25, bf16[3,128,384]{1,2,0:T(8,128)(2,1)S(1)} %get-tuple-element.16, bf16[3,128,384]{2,1,0:T(8,128)(2,1)S(1)} %get-tuple-element.23, bf16[3,128,384]{2,1,0:T(8,128)(2,1)S(1)} %get-tuple-element.22), kind=kOutput, calls=%fused_computation.7 | convolution fusion | flops 459767808 | bytes 5013504 | tf_op jit(solution)/shard_map/tsi,tsj->itj/dot_general | solution.py:53
  18.9 142.3 %all-reduce.3.cloned.1.call-done = f32[384,3,768]{0,2,1:T(8,128)} async-done(((f32[384,3,768]{0,2,1:T(8,128)}), f32[384,3,768]{0,2,1:T(8,128)}) %all-reduce.3.cloned.1.call-update) | async-done | bytes 3538960 | tf_op jit(solution)/shard_map/psum | solution.py:52
  161.2 2.2 convert_element_type.30
  163.6 0.6 gather_fusion
  164.3 0.5 compare_and_fusion.1
  164.9 2.0 constant_dynamic-slice_fusion
  166.9 1.1 copy.33
  168.0 2.4 %pad_maximum_fusion = bf16[384,6,768]{0,2,1:T(8,128)(2,1)S(1)} fusion(bf16[384,3,768]{0,2,1:T(8,128)(2,1)} %collective-permute-done, bf16[384,3,768]{0,2,1:T(8,128)(2,1)} %copy-done.1), kind=kLoop, calls=%fused_computation.6 | loop fusion | flops 1769472 | bytes 7077888 | tf_op jit(solution)/shard_map/concatenate | solution.py:60
  170.4 2.1 gather_fusion.1
  172.5 2.8 %fusion.4 = f32[3,256,384]{2,1,0:T(8,128)S(1)} fusion(bf16[3,384,768]{1,2,0:T(8,128)(2,1)} %gather_fusion.1, pred[3]{0:T(512)(128)(4,1)} %compare_and_fusion.1, bf16[3,128,384]{1,2,0:T(8,128)(2,1)} %copy-done.3, bf16[3,128,384]{1,2,0:T(8,128)(2,1)} %copy-done.2, bf16[3,128,384]{1,2,0:T(8,128)(2,1)} %get-tuple-element.21), kind=kOutput, calls=%fused_computation.12 | convolution fusion | flops 458883072 | bytes 3833859 | tf_op jit(solution)/shard_map/tsj,itj->tsi/dot_general | solution.py:61
  175.3 0.2 fusion.29
  175.6 34.7 %all-reduce = (f32[3,384]{1,0:T(4,128)S(1)}, f32[3,384]{1,0:T(4,128)S(1)}) all-reduce(f32[3,384]{1,0:T(4,128)S(1)} %get-tuple-element.27, f32[3,384]{1,0:T(4,128)S(1)} %get-tuple-element.26), channel_id=1, replica_groups=mesh['group'=2,'space'=8,'tm'=2] {'space'}, use_global_device_ids=true, to_apply=%region_2.4 | all-reduce | flops 2304 | bytes 18432 | tf_op jit(solution)/shard_map/psum | solution.py:69
  210.6 1.5 scatter_custom_fusion
  212.1 1.6 scatter_fusion
  213.7 0.8 copy.34
  (46 shorter events, 1.6 us)
Async XLA Ops:
  7.2 156.4 %copy-start = (s32[6]{0:T(128)S(1)}, s32[6]{0:T(128)}, u32[]{:S(2)}) copy-start(s32[6]{0:T(128)} %param.10) | copy-start | bytes 76
  7.2 1.4 copy-start.9
  7.2 154.0 %all-reduce.3.cloned.1.call-start = ((), (), s32[]{:S(2)}) async-start(), calls=%async_computation | async-start | bytes 7077888 | tf_op jit(solution)/shard_map/psum | solution.py:52
  8.4 1.5 copy-start.10
  8.4 1.7 copy-start.8
  8.6 1.6 copy-start.2
  8.9 1.3 copy-start.3
  15.5 0.7 copy-start.4
  15.5 0.8 copy-start.6
  163.4 4.6 %copy-start.1 = (bf16[384,3,768]{0,2,1:T(8,128)(2,1)}, bf16[384,3,768]{0,2,1:T(8,128)(2,1)S(1)}, u32[]{:S(2)}) copy-start(bf16[384,3,768]{0,2,1:T(8,128)(2,1)S(1)} %convert_element_type.30) | copy-start | bytes 5308420
  163.4 4.6 %collective-permute-start = (bf16[384,3,768]{0,2,1:T(8,128)(2,1)S(1)}, bf16[384,3,768]{0,2,1:T(8,128)(2,1)}, u32[]{:S(2)}, u32[]{:S(2)}) collective-permute-start(bf16[384,3,768]{0,2,1:T(8,128)(2,1)S(1)} %convert_element_type.30), channel_id=1, source_target_pairs={{1,0},{0,1},{3,2},{2,3},{5,4},{4,5},{7,6},{6,7},{9,8},{8,9},{11,10... | collective-permute-start | bytes 5308424 | tf_op jit(solution)/shard_map/ppermute | solution.py:14
  172.5 2.8 %copy-start.5 = (bf16[3,128,384]{2,1,0:T(8,128)(2,1)S(1)}, bf16[3,128,384]{2,1,0:T(8,128)(2,1)}, u32[]{:S(2)}) copy-start(bf16[3,128,384]{2,1,0:T(8,128)(2,1)} %copy-done.4) | copy-start | bytes 884740
  172.5 2.8 %copy-start.7 = (bf16[3,128,384]{2,1,0:T(8,128)(2,1)S(1)}, bf16[3,128,384]{2,1,0:T(8,128)(2,1)}, u32[]{:S(2)}) copy-start(bf16[3,128,384]{2,1,0:T(8,128)(2,1)} %copy-done.6) | copy-start | bytes 884740
Sparse Core Ops, SparseCore 0:
  19.0 142.1 all-reduce.2
where the time goes:
time: 222 us; the launch traced here: 221 us
  waiting for transfers between devices  142 us (64%)
  blocking collectives  34.7 us (16%)
  local copies, waits for them, and re-layouts  17.8 us (8%)
  between operations  14.3 us (6%)
  other arithmetic  6.68 us (3%)
  matrix products  5.36 us (2%)
    psum x1, waiting for transfers between devices, shards(): lax.psum(jnp.einsum('tsi,tsj->itj', left, right, preferred_element_type=j...  142 us
    psum x1, blocking collectives, shards(): total_real, total_imag = lax.psum((over_real, over_imag), 'space')  34.7 us
  transfers between devices with their start and end apart: 2, of which 1 were waited for; matrix products, arithmetic and copies ran while one was open for 2% of the time, Pallas kernels for 0%

commit v1 on v0

v1 whole, which is shorter than its diff:
```python
import functools
import math

import jax
import jax.numpy as jnp
from jax import lax
from jax.experimental import pallas as pl
from jax.experimental.pallas import tpu as pltpu
from jax.sharding import PartitionSpec as P

PHASES = 96
MESH = pl.DeviceIdType.MESH
F32 = jnp.float32
BF16 = jnp.bfloat16


def transposed_dot(left, right):
    return lax.dot_general(left, right, (((0,), (0,)), ((), ())), preferred_element_type=F32)


def kernel(
    nslices,
    w_ref, v_ref, ph_ref, seq_ref, own_ref,
    strips_ref, margin_ref,
    wx, vx, phs, phx, trig, left, right, part, tx0, tx1, rx0, rx1, fields, gfin0, gfin1, cols, tile, gathered, place, hot, chosen0, chosen1,
    xs_sem, xr_sem, zs_sem, zr_sem, ms_sem, mr_sem, ts_sem, tr_sem, as_sem, ar_sem,
):
    tdev, sdev, width = w_ref.shape
    n = width // 2
    block = strips_ref.shape[1]
    s = lax.axis_index("space")
    c = lax.axis_index("tm")
    nspace = lax.axis_size("space")
    z, x = s // 2, s % 2
    peer = 2 * z + (1 - x)
    scale_sites = 1.0 / math.sqrt(sdev * nspace)
    scale_modes = 1.0 / math.sqrt(2 * n)
    mine, other = 2 * x, 2 - 2 * x
    is_end = jnp.logical_or(z == 0, z == 3)
    is_mid = jnp.logical_not(is_end)
    low = z < 2

    barrier = pltpu.get_barrier_semaphore()
    for k in range(1, nspace):
        pl.semaphore_signal(barrier, inc=1, device_id={"space": (s + k) % nspace}, device_id_type=MESH)
    pl.semaphore_signal(barrier, inc=1, device_id={"tm": 1 - c}, device_id_type=MESH)
    phs[...] = jnp.broadcast_to(ph_ref[...].astype(F32), phs.shape)
    pl.semaphore_wait(barrier, nspace)

    def to(src, dst, ssem, rsem, **where):
        return pltpu.make_async_remote_copy(src, dst, ssem, rsem, device_id=where, device_id_type=MESH)

    swaps = [to(phs, phx, xs_sem.at[0], xr_sem.at[0], space=peer)]
    for j, t in ((0, other), (1, 1)):
        swaps.append(to(w_ref.at[t], wx.at[j], xs_sem.at[1 + 2 * j], xr_sem.at[1 + 2 * j], space=peer))
        swaps.append(to(v_ref.at[t], vx.at[j], xs_sem.at[2 + 2 * j], xr_sem.at[2 + 2 * j], space=peer))
    for swap in swaps:
        swap.start()

    def set_trig(q, row):
        angle = row * (2.0 * math.pi / PHASES)
        for k, fn in ((0, jnp.cos), (1, jnp.sin)):
            value = fn(angle)[0:1, :]
            trig[q, k] = jnp.transpose(jnp.broadcast_to(value, (sdev, sdev)))

    def build(q, w, v):
        left[:sdev] = jnp.dot(w[:, :n], hot[...], preferred_element_type=F32).astype(BF16)
        left[sdev:] = jnp.dot(w[:, n:], hot[...], preferred_element_type=F32).astype(BF16)
        for k in range(n // 128):
            lanes = slice(k * 128, (k + 1) * 128)
            vr, vi = v[:, k * 128:(k + 1) * 128], v[:, n + k * 128:n + (k + 1) * 128]
            fr, fi = vr.astype(F32), vi.astype(F32)
            cosv, sinv = trig[q, 0], trig[q, 1]
            pr = (cosv * fr + sinv * fi).astype(BF16)
            pi = (cosv * fi - sinv * fr).astype(BF16)
            for m, (re, im) in enumerate(((pr, pi), (vr, vi))):
                right[m, :sdev, lanes] = re
                right[m, :sdev, n + k * 128:n + (k + 1) * 128] = im
                right[m, sdev:, lanes] = im
                right[m, sdev:, n + k * 128:n + (k + 1) * 128] = -re

    mode = lax.broadcasted_iota(jnp.int32, (n, n), 0)
    spot = lax.broadcasted_iota(jnp.int32, (n, n), 1)
    wanted = jnp.full((n, n), -1, jnp.int32)
    for p in range(nspace):
        inside = jnp.logical_and(spot >= p * block, spot < (p + 1) * block)
        wanted = jnp.where(inside, own_ref[p] * block + spot - p * block, wanted)
    hot[...] = jnp.where(mode == wanted, 1.0, 0.0).astype(BF16)

    set_trig(0, phs[...])
    for j, t in ((0, mine), (1, 1)):
        build(0, w_ref.at[t], v_ref.at[t])
        for m in range(2):
            part[j, m] = transposed_dot(left[...], right[m]) * scale_sites

    lane = lax.broadcasted_iota(jnp.int32, (128, n), 1)
    row = lax.broadcasted_iota(jnp.int32, (128, n), 0)
    for zz in range(nspace // 2):
        first = own_ref[2 * zz] * block + row
        second = own_ref[2 * zz + 1] * block + row - block
        spot = jnp.where(row < block, first, jnp.where(row < 2 * block, second, -1))
        place[zz] = jnp.where(spot == lane, 1.0, 0.0)

    tx, rx = (tx0, tx1), (rx0, rx1)

    def rows_of(j, m, far, k):
        zd = jnp.where(low, far, 3 - far)
        at = (2 * zd + (k if j == 0 else x)) * block
        return part[j, m, pl.ds(pl.multiple_of(at, 16), block), :]

    nk = (2, 1)

    def hop(j, m, slot, dst_slot, znext):
        return to(
            tx[j].at[m, slot], rx[j].at[m, dst_slot], zs_sem.at[j, m, slot], zr_sem.at[j, m, dst_slot],
            space=2 * znext + x,
        )

    def got(j, m, slot):
        hop(j, m, 0, slot, z).wait_recv()

    inner = jnp.where(low, 1, 2)
    outer = jnp.where(low, 0, 3)

    def send(j, m, slot, dst_slot, far, znext, add):
        for k in range(nk[j]):
            value = rows_of(j, m, far, k)
            if add is not None:
                value = value + rx[j][m, add, k * block:(k + 1) * block, :].astype(F32)
            tx[j][m, slot, k * block:(k + 1) * block, :] = value.astype(BF16)
        hop(j, m, slot, dst_slot, znext).start()

    def reduce(j, m):
        @pl.when(is_end)
        def _():
            for i, far in enumerate((3, 2, 1)):
                send(j, m, i, i, far, inner, None)

        @pl.when(is_mid)
        def _():
            for i, far in enumerate((3, 2)):
                got(j, m, i)
                send(j, m, i, 3 + i, far, 3 - z, i)
            got(j, m, 3)
            send(j, m, 2, 0, 0, outer, 3)

    def finish(j, m, store):
        @pl.when(is_end)
        def _():
            got(j, m, 0)
            for k in range(nk[j]):
                store(k, rows_of(j, m, 0, k) + rx[j][m, 0, k * block:(k + 1) * block, :].astype(F32))

        @pl.when(is_mid)
        def _():
            got(j, m, 2)
            got(j, m, 4)
            for k in range(nk[j]):
                rows = slice(k * block, (k + 1) * block)
                store(k, rows_of(j, m, 1, k) + rx[j][m, 2, rows, :].astype(F32) + rx[j][m, 4, rows, :].astype(F32))

    def store_field0(k, value):
        fields[3 * c + mine, k * block:(k + 1) * block, :] = value.astype(BF16)

        @pl.when(x == k)
        def _():
            strips_ref[mine] = value

    def store_field1(k, value):
        fields[3 * c + 1, pl.ds(pl.multiple_of(x * block, 16), block), :] = value.astype(BF16)
        strips_ref[1] = value

    def store_g0(k, value):
        gfin0[k * block:(k + 1) * block, :] = value

    def store_g1(k, value):
        gfin1[...] = value

    swaps[0].wait_recv()
    set_trig(1, phx[...])
    for j in range(2):
        swaps[1 + 2 * j].wait_recv()
        swaps[2 + 2 * j].wait_recv()
        build(1, wx.at[j], vx.at[j])
        part[j, 0] += transposed_dot(left[...], right[0]) * scale_sites
        reduce(j, 0)
        part[j, 1] += transposed_dot(left[...], right[1]) * scale_sites
    for j in range(2):
        reduce(j, 1)

    half = pl.ds(pl.multiple_of(x * block, 16), block)
    half_peer = pl.ds(pl.multiple_of((1 - x) * block, 16), block)
    give0 = to(fields.at[3 * c + mine], fields.at[3 * c + mine], ms_sem.at[0], mr_sem.at[0], space=peer)
    give1 = to(fields.at[3 * c + 1, half], fields.at[3 * c + 1, half], ms_sem.at[1], mr_sem.at[1], space=peer)
    finish(0, 0, store_field0)
    give0.start()
    finish(1, 0, store_field1)
    give1.start()
    give0.wait_recv()
    give1.wait_recv()
    sibling = to(
        fields.at[pl.ds(3 * c, 3)], fields.at[pl.ds(3 * c, 3)], ts_sem.at[0], tr_sem.at[0], tm=1 - c
    )
    sibling.start()
    strips_ref[other] = fields[3 * c + other, half, :].astype(F32)
    sibling.wait_recv()

    def weight(t, k):
        at = 3 * c + t
        there = at + seq_ref[at]
        return jnp.where(jnp.logical_or(there == k, there == k + nslices), 1.0, 0.0)

    chosen0[...] = sum(weight(mine, k) * fields[k].astype(F32) for k in range(nslices))
    chosen1[...] = sum(weight(1, k) * fields[k, half, :].astype(F32) for k in range(nslices))
    finish(0, 1, store_g0)
    finish(1, 1, store_g1)

    def margins(g, field):
        gr, gi = g[:, :n], g[:, n:]
        mr, mi = field[:, :n], field[:, n:]
        re = jnp.sum(mr * gr - mi * gi, axis=1, keepdims=True) * scale_modes
        im = jnp.sum(mr * gi + mi * gr, axis=1, keepdims=True) * scale_modes
        return re, im

    cols[...] = jnp.zeros_like(cols)
    at = lax.broadcasted_iota(jnp.int32, (2 * block, 128), 1)
    re, im = margins(gfin0[...], chosen0[...])
    cols[:2 * block] = jnp.where(at == 0, re, 0.0) + jnp.where(at == 1, im, 0.0)
    re, im = margins(gfin1[...], chosen1[...])
    at = lax.broadcasted_iota(jnp.int32, (block, 128), 1)
    cols[half] += jnp.where(at == 2, re, 0.0) + jnp.where(at == 3, im, 0.0)
    tile[...] = jnp.transpose(cols[...])[:8]

    shares = []
    for k in range(1, nspace):
        share = to(tile, gathered.at[s], as_sem.at[k], ar_sem.at[s], space=(s + k) % nspace)
        share.start()
        shares.append(share)
    gathered[s] = tile[...]
    for k in range(1, nspace):
        origin = (s + k) % nspace
        to(tile, gathered.at[origin], as_sem.at[k], ar_sem.at[origin], space=origin).wait_recv()
    total = jnp.zeros((16, n), F32)
    for zz in range(nspace // 2):
        both = jnp.concatenate([gathered[2 * zz], gathered[2 * zz + 1]], axis=0)
        total += jnp.dot(both, place[zz], precision=lax.Precision.HIGHEST, preferred_element_type=F32)
    margin_ref[0:1, :n] = total[0:1]
    margin_ref[0:1, n:] = total[1:2]
    margin_ref[1:2, :n] = total[2:3] + total[10:11]
    margin_ref[1:2, n:] = total[3:4] + total[11:12]
    margin_ref[2:3, :n] = total[8:9]
    margin_ref[2:3, n:] = total[9:10]

    for swap in swaps:
        swap.wait_send()
    for j in range(2):
        for m in range(2):
            for slot in range(3):
                hop(j, m, slot, 0, z).wait_send()
    give0.wait_send()
    give1.wait_send()
    sibling.wait_send()
    for share in shares:
        share.wait_send()


def fused(w_modes, v_modes, phase_index, seq_offset, owner_block):
    tdev, sdev, width = w_modes.shape
    n = width // 2
    nspace = lax.axis_size("space")
    ntm = lax.axis_size("tm")
    block = n // nspace
    vmem = pl.BlockSpec(memory_space=pltpu.VMEM)
    smem = pl.BlockSpec(memory_space=pltpu.SMEM)
    dma = pltpu.SemaphoreType.DMA
    strips, margin = pl.pallas_call(
        functools.partial(kernel, tdev * ntm),
        out_shape=(
            jax.ShapeDtypeStruct((tdev, block, width), F32),
            jax.ShapeDtypeStruct((tdev, width), F32),
        ),
        in_specs=[vmem, vmem, vmem, smem, smem],
        out_specs=(vmem, vmem),
        scratch_shapes=[
            pltpu.VMEM((2, sdev, width), BF16),
            pltpu.VMEM((2, sdev, width), BF16),
            pltpu.VMEM((8, sdev), F32),
            pltpu.VMEM((8, sdev), F32),
            pltpu.VMEM((2, 2, sdev, sdev), F32),
            pltpu.VMEM((2 * sdev, n), BF16),
            pltpu.VMEM((2, 2 * sdev, width), BF16),
            pltpu.VMEM((2, 2, n, width), F32),
            pltpu.VMEM((2, 3, 2 * block, width), BF16),
            pltpu.VMEM((2, 3, block, width), BF16),
            pltpu.VMEM((2, 5, 2 * block, width), BF16),
            pltpu.VMEM((2, 5, block, width), BF16),
            pltpu.VMEM((tdev * ntm, 2 * block, width), BF16),
            pltpu.VMEM((2 * block, width), F32),
            pltpu.VMEM((block, width), F32),
            pltpu.VMEM((128, 128), F32),
            pltpu.VMEM((8, 128), F32),
            pltpu.VMEM((nspace, 8, 128), F32),
            pltpu.VMEM((nspace // 2, 128, n), F32),
            pltpu.VMEM((n, n), BF16),
            pltpu.VMEM((2 * block, width), F32),
            pltpu.VMEM((block, width), F32),
            dma((5,)),
            dma((5,)),
            dma((2, 2, 3)),
            dma((2, 2, 5)),
            dma((2,)),
            dma((2,)),
            dma((1,)),
            dma((1,)),
            dma((nspace,)),
            dma((nspace,)),
        ],
        compiler_params=pltpu.CompilerParams(
            collective_id=0, has_side_effects=True, vmem_limit_bytes=48 * 1024 * 1024
        ),
        cost_estimate=pl.CostEstimate(
            flops=16 * tdev * sdev * n * n, bytes_accessed=4 * tdev * sdev * width, transcendentals=0
        ),
    )(w_modes, v_modes, phase_index.reshape(1, sdev), seq_offset, owner_block)
    return jnp.transpose(strips, (1, 0, 2)), margin


def plain(w_modes, v_modes, phase_index, seq_offset, owner_block):
    tdev, sdev, width = w_modes.shape
    nmode = width // 2
    nspace = lax.axis_size("space")
    ntm = lax.axis_size("tm")
    block = nmode // nspace
    total_slices = tdev * ntm
    scale_sites = 1.0 / math.sqrt(sdev * nspace)
    scale_modes = 1.0 / math.sqrt(2 * nmode)
    order = (owner_block[:, None] * block + jnp.arange(block, dtype=jnp.int32)[None, :]).reshape(-1)
    spots = order[:, None] == jnp.arange(nmode, dtype=jnp.int32)[None, :]
    hot = spots.astype(BF16)
    exact = spots.astype(F32)
    w_real = jnp.einsum("tsm,km->tsk", w_modes[:, :, :nmode], hot)
    w_imag = jnp.einsum("tsm,km->tsk", w_modes[:, :, nmode:], hot)
    v_real, v_imag = v_modes[:, :, :nmode], v_modes[:, :, nmode:]
    left = jnp.concatenate([w_real, w_imag], axis=1)
    angle = phase_index.astype(F32) * (2.0 * math.pi / PHASES)
    cosv = jnp.cos(angle)[None, :, None]
    sinv = jnp.sin(angle)[None, :, None]
    fr, fi = v_real.astype(F32), v_imag.astype(F32)
    ph_real = (cosv * fr + sinv * fi).astype(BF16)
    ph_imag = (cosv * fi - sinv * fr).astype(BF16)

    def field(real, imag):
        right = jnp.concatenate(
            [jnp.concatenate([real, imag], axis=2), jnp.concatenate([imag, -real], axis=2)], axis=1
        )
        sums = jnp.einsum("tsi,tsj->itj", left, right, preferred_element_type=F32) * scale_sites
        return lax.psum_scatter(sums, "space", scatter_dimension=0, tiled=True)

    strips = field(ph_real, ph_imag)
    g = field(v_real, v_imag)
    rounded = strips.astype(BF16)
    both = lax.all_gather(rounded, "tm", axis=1, tiled=True)
    mine = lax.axis_index("tm") * tdev + jnp.arange(tdev, dtype=jnp.int32)
    every = jnp.arange(total_slices, dtype=jnp.int32)
    offset = jnp.sum(jnp.where(mine[:, None] == every[None, :], seq_offset[None, :], 0), axis=1)
    target = (mine + offset) % total_slices
    pick = (target[:, None] == every[None, :]).astype(BF16)
    chosen = jnp.einsum("iaj,ta->itj", both, pick, preferred_element_type=F32)
    cr, ci = chosen[:, :, :nmode], chosen[:, :, nmode:]
    gr, gi = g[:, :, :nmode], g[:, :, nmode:]
    over = jnp.concatenate(
        [jnp.sum(cr * gr - ci * gi, axis=2), jnp.sum(cr * gi + ci * gr, axis=2)], axis=1
    ) * scale_modes
    rows = lax.all_gather(over, "space", axis=0, tiled=True)
    margin = jnp.einsum("kt,km->tm", rows, exact, precision=lax.Precision.HIGHEST)
    return strips, jnp.concatenate([margin[:tdev], margin[tdev:]], axis=1)


def shards(w_modes, v_modes, phase_index, seq_offset, owner_block):
    tdev, sdev, width = w_modes.shape
    nmode = width // 2
    nspace = lax.axis_size("space")
    fits = (
        tdev == 3 and lax.axis_size("tm") == 2 and nspace == 8 and sdev == 128
        and nmode % 128 == 0 and (nmode // nspace) % 16 == 0 and 2 * (nmode // nspace) <= 128
    )
    return (fused if fits else plain)(w_modes, v_modes, phase_index, seq_offset, owner_block)


def solution(mesh):
    in_specs = (
        P(("group", "tm"), "space", None),
        P(("group", "tm"), "space", None),
        P("space"),
        P(),
        P(),
    )
    out_specs = (P("space", ("group", "tm"), None), P(("group", "tm"), None))
    return jax.shard_map(shards, mesh=mesh, in_specs=in_specs, out_specs=out_specs, check_vma=False)
```

time: 222 us -> 63 us (0.28)
  waiting for transfers between devices: 142 us -> 0 us
  Pallas kernels: 0 us -> 57.5 us
  blocking collectives: 34.7 us -> 0 us
  local copies, waits for them, and re-layouts: 17.8 us -> 4.15 us
  between operations: 14.3 us -> 0.67 us
  other arithmetic: 6.68 us -> 0 us
  matrix products: 5.36 us -> 0 us
    psum x1 -> x0, waiting for transfers between devices: 142 us -> none  [shards(): lax.psum(jnp.einsum('tsi,tsj->itj', left, right, preferred_element_type=j...]
    pallas_call x0 -> x1, Pallas kernels: none -> 57.5 us  [fused(): pl.pallas_call(functools.partial(kernel, tdev * ntm), out_shape=(jax.Shap...]
    psum x1 -> x0, blocking collectives: 34.7 us -> none  [shards(): total_real, total_imag = lax.psum((over_real, over_imag), 'space')]
    gather x6 -> x0, local copies, waits for them, and re-layouts: 7.38 us -> none  [the longest x2 2.32 us: shards(): w_real = jnp.take(w_modes[:, :, :nmode], order, axis=2)]
    dot_general x2 -> x0, matrix products: 5.36 us -> none  [the longest x1 2.76 us: shards(): jnp.einsum('tsj,itj->tsi', v_two, chosen, preferred_element_type=jnp.floa...]
    scatter x2 -> x0, local copies, waits for them, and re-layouts: 3.14 us -> none  [shards(): margin.at[:, order].set(total_real).at[:, order + nmode].set(total_imag)]
    concatenate x1 -> x0, other arithmetic: 2.41 us -> none  [shards(): chosen = jnp.take(jnp.concatenate(pieces, axis=1), pick, axis=1)]
    convert_element_type x2 -> x0, other arithmetic: 2.31 us -> none  [the longest x1 2.19 us: shards(): rounded = full.astype(jnp.bfloat16)]
  transfers between devices with their start and end apart: 2 -> 0, of which waited for: 1 -> 0; matrix products, arithmetic and copies ran while one was open for 2% -> 0% of each run, Pallas kernels for 0% -> 0%
where the time goes in v1:
time: 63 us; the launch traced here: 62.3 us
  Pallas kernels  57.5 us (91%)
  local copies, waits for them, and re-layouts  4.15 us (7%)
  between operations  0.67 us (1%)
    pallas_call x1, Pallas kernels, fused(): pl.pallas_call(functools.partial(kernel, tdev * ntm), out_shape=(jax.Shap...  57.5 us
    unnamed x12, local copies, waits for them, and re-layouts  4.15 us

profile of v1, /device:TPU:0, one launch (start us, length us, event | category | flops | bytes accessed | tf_op | source)
XLA Modules:
  0.0 62.3 jit_solution(13915305563495795397)
XLA Ops:
  0.6 0.0 copy-start.4
  0.6 0.0 copy-start.3
  0.7 0.0 copy-start.2
  0.7 0.6 %copy-done.4 = s32[8]{0:T(128)S(1)} copy-done((s32[8]{0:T(128)S(1)}, s32[8]{0:T(128)}, u32[]{:S(2)}) %copy-start.4) | copy-done | bytes 56
  1.3 0.0 copy-done.3
  1.3 0.0 copy-done.2
  1.3 0.0 copy-start
  1.3 1.1 %copy-done = bf16[3,128,768]{2,1,0:T(8,128)(2,1)S(1)} copy-done((bf16[3,128,768]{2,1,0:T(8,128)(2,1)S(1)}, bf16[3,128,768]{2,1,0:T(8,128)(2,1)}, u32[]{:S(2)}) %copy-start) | copy-done | bytes 589848
  2.4 0.0 copy-start.1
  2.4 1.1 %copy-done.1 = bf16[3,128,768]{2,1,0:T(8,128)(2,1)S(1)} copy-done((bf16[3,128,768]{2,1,0:T(8,128)(2,1)S(1)}, bf16[3,128,768]{2,1,0:T(8,128)(2,1)}, u32[]{:S(2)}) %copy-start.1) | copy-done | bytes 589848
  3.4 57.5 %shard_map.68 = (f32[3,48,768]{2,1,0:T(8,128)S(1)}, f32[3,768]{1,0:T(4,128)S(1)}) custom-call(bf16[3,128,768]{2,1,0:T(8,128)(2,1)S(1)} %copy-done, bf16[3,128,768]{2,1,0:T(8,128)(2,1)S(1)} %copy-done.1, s32[1,128]{1,0:T(1,128)S(1)} %bitcast.3, s32[6]{0:T(128)S(1)} %copy-done.3, s32[8]{0:T(128)S(1)} %copy-done.4), custom_call_target="tpu_custom_call" | custom-call | flops 905969664 | bytes 1179648 | tf_op jit(solution)/shard_map/pallas_call | solution.py:276
  61.0 0.8 %copy.9 = f32[48,3,768]{2,0,1:T(8,128)} copy(f32[48,3,768]{2,0,1:T(8,128)S(1)} %bitcast.2) | data formatting | bytes 884736
  61.7 0.6 copy.10
Async XLA Ops:
  0.6 0.7 %copy-start.4 = (s32[8]{0:T(128)S(1)}, s32[8]{0:T(128)}, u32[]{:S(2)}) copy-start(s32[8]{0:T(128)} %own_ref.1) | copy-start | bytes 100
  0.6 0.7 %copy-start.3 = (s32[6]{0:T(128)S(1)}, s32[6]{0:T(128)}, u32[]{:S(2)}) copy-start(s32[6]{0:T(128)} %seq_ref.1) | copy-start | bytes 76
  0.7 0.7 %copy-start.2 = (s32[128]{0:T(128)S(1)}, s32[128]{0:T(128)}, u32[]{:S(2)}) copy-start(s32[128]{0:T(128)} %param.7) | copy-start | bytes 1540
  1.3 1.1 %copy-start = (bf16[3,128,768]{2,1,0:T(8,128)(2,1)S(1)}, bf16[3,128,768]{2,1,0:T(8,128)(2,1)}, u32[]{:S(2)}) copy-start(bf16[3,128,768]{2,1,0:T(8,128)(2,1)} %w_ref.1) | copy-start | bytes 1769476
  2.4 1.1 %copy-start.1 = (bf16[3,128,768]{2,1,0:T(8,128)(2,1)S(1)}, bf16[3,128,768]{2,1,0:T(8,128)(2,1)}, u32[]{:S(2)}) copy-start(bf16[3,128,768]{2,1,0:T(8,128)(2,1)} %v_ref.1) | copy-start | bytes 1769476

commit v2 on v1

--- a/solution.py
+++ b/solution.py
@@ -22,7 +22,7 @@
     nslices,
     w_ref, v_ref, ph_ref, seq_ref, own_ref,
     strips_ref, margin_ref,
-    wx, vx, phs, phx, trig, left, right, part, tx0, tx1, rx0, rx1, fields, gfin0, gfin1, cols, tile, gathered, place, hot, chosen0, chosen1,
+    wx, vx, phs, phx, trig, left, right, part, tx0, tx1, rx0, rx1, fields, gfin0, gfin1, cols, tile, gathered, place, hot, chosen0, chosen1, wo, vo, lo_sem,
     xs_sem, xr_sem, zs_sem, zr_sem, ms_sem, mr_sem, ts_sem, tr_sem, as_sem, ar_sem,
 ):
     tdev, sdev, width = w_ref.shape
@@ -40,6 +40,13 @@
     is_mid = jnp.logical_not(is_end)
     low = z < 2
 
+    loads = []
+    for j, t in ((0, mine), (1, 1)):
+        loads.append(pltpu.make_async_copy(w_ref.at[t], wo.at[j], lo_sem.at[2 * j]))
+        loads.append(pltpu.make_async_copy(v_ref.at[t], vo.at[j], lo_sem.at[2 * j + 1]))
+    for load in loads:
+        load.start()
+
     barrier = pltpu.get_barrier_semaphore()
     for k in range(1, nspace):
         pl.semaphore_signal(barrier, inc=1, device_id={"space": (s + k) % nspace}, device_id_type=MESH)
@@ -54,7 +61,7 @@
     for j, t in ((0, other), (1, 1)):
         swaps.append(to(w_ref.at[t], wx.at[j], xs_sem.at[1 + 2 * j], xr_sem.at[1 + 2 * j], space=peer))
         swaps.append(to(v_ref.at[t], vx.at[j], xs_sem.at[2 + 2 * j], xr_sem.at[2 + 2 * j], space=peer))
-    for swap in swaps:
+    for swap in swaps[:3]:
         swap.start()
 
     def set_trig(q, row):
@@ -88,8 +95,10 @@
     hot[...] = jnp.where(mode == wanted, 1.0, 0.0).astype(BF16)
 
     set_trig(0, phs[...])
-    for j, t in ((0, mine), (1, 1)):
-        build(0, w_ref.at[t], v_ref.at[t])
+    for j in range(2):
+        loads[2 * j].wait()
+        loads[2 * j + 1].wait()
+        build(0, wo.at[j], vo.at[j])
         for m in range(2):
             part[j, m] = transposed_dot(left[...], right[m]) * scale_sites
 
@@ -176,6 +185,10 @@
     def store_g1(k, value):
         gfin1[...] = value
 
+    for swap in swaps[:3]:
+        swap.wait_send()
+    for swap in swaps[3:]:
+        swap.start()
     swaps[0].wait_recv()
     set_trig(1, phx[...])
     for j in range(2):
@@ -251,7 +264,7 @@
     margin_ref[2:3, :n] = total[8:9]
     margin_ref[2:3, n:] = total[9:10]
 
-    for swap in swaps:
+    for swap in swaps[3:]:
         swap.wait_send()
     for j in range(2):
         for m in range(2):
@@ -271,6 +284,7 @@
     ntm = lax.axis_size("tm")
     block = n // nspace
     vmem = pl.BlockSpec(memory_space=pltpu.VMEM)
+    hbm = pl.BlockSpec(memory_space=pltpu.HBM)
     smem = pl.BlockSpec(memory_space=pltpu.SMEM)
     dma = pltpu.SemaphoreType.DMA
     strips, margin = pl.pallas_call(
@@ -279,7 +293,7 @@
             jax.ShapeDtypeStruct((tdev, block, width), F32),
             jax.ShapeDtypeStruct((tdev, width), F32),
         ),
-        in_specs=[vmem, vmem, vmem, smem, smem],
+        in_specs=[hbm, hbm, vmem, smem, smem],
         out_specs=(vmem, vmem),
         scratch_shapes=[
             pltpu.VMEM((2, sdev, width), BF16),
@@ -304,6 +318,9 @@
             pltpu.VMEM((n, n), BF16),
             pltpu.VMEM((2 * block, width), F32),
             pltpu.VMEM((block, width), F32),
+            pltpu.VMEM((2, sdev, width), BF16),
+            pltpu.VMEM((2, sdev, width), BF16),
+            dma((4,)),
             dma((5,)),
             dma((5,)),
             dma((2, 2, 3)),

time: 63 us -> 64.6 us (1.025)
  Pallas kernels: 57.5 us -> 59.1 us
    pallas_call x1, Pallas kernels: 57.5 us -> 59.1 us  [fused(): pl.pallas_call(functools.partial(kernel, tdev * ntm), out_shape=(jax.Shap...]
where the time goes in v2:
time: 64.6 us; the launch traced here: 63.9 us
  Pallas kernels  59.1 us (91%)
  local copies, waits for them, and re-layouts  4.15 us (6%)
  between operations  0.67 us (1%)
    pallas_call x1, Pallas kernels, fused(): pl.pallas_call(functools.partial(kernel, tdev * ntm), out_shape=(jax.Shap...  59.1 us
    unnamed x12, local copies, waits for them, and re-layouts  4.15 us

profile of v2, /device:TPU:0, one launch (start us, length us, event | category | flops | bytes accessed | tf_op | source)
XLA Modules:
  0.0 63.9 jit_solution(9141474615755663801)
XLA Ops:
  0.6 0.0 copy-start.4
  0.6 0.0 copy-start.3
  0.7 0.0 copy-start.2
  0.7 0.6 copy-done.4
  1.3 0.0 copy-done.3
  1.3 0.0 copy-done.2
  1.3 0.0 copy-start
  1.3 1.1 %copy-done = bf16[3,128,768]{2,1,0:T(8,128)(2,1)S(1)} copy-done((bf16[3,128,768]{2,1,0:T(8,128)(2,1)S(1)}, bf16[3,128,768]{2,1,0:T(8,128)(2,1)}, u32[]{:S(2)}) %copy-start) | copy-done | bytes 589848
  2.4 0.0 copy-start.1
  2.4 1.1 %copy-done.1 = bf16[3,128,768]{2,1,0:T(8,128)(2,1)S(1)} copy-done((bf16[3,128,768]{2,1,0:T(8,128)(2,1)S(1)}, bf16[3,128,768]{2,1,0:T(8,128)(2,1)}, u32[]{:S(2)}) %copy-start.1) | copy-done | bytes 589848
  3.4 59.1 %shard_map.68 = (f32[3,48,768]{2,1,0:T(8,128)S(1)}, f32[3,768]{1,0:T(4,128)S(1)}) custom-call(bf16[3,128,768]{2,1,0:T(8,128)(2,1)S(1)} %copy-done, bf16[3,128,768]{2,1,0:T(8,128)(2,1)S(1)} %copy-done.1, s32[1,128]{1,0:T(1,128)S(1)} %bitcast.3, s32[6]{0:T(128)S(1)} %copy-done.3, s32[8]{0:T(128)S(1)} %copy-done.4), custom_call_target="tpu_custom_call" | custom-call | flops 905969664 | bytes 1179648 | tf_op jit(solution)/shard_map/pallas_call | solution.py:290
  62.6 0.8 %copy.9 = f32[48,3,768]{2,0,1:T(8,128)} copy(f32[48,3,768]{2,0,1:T(8,128)S(1)} %bitcast.2) | data formatting | bytes 884736
  63.3 0.6 copy.10
Async XLA Ops:
  0.6 0.7 %copy-start.4 = (s32[8]{0:T(128)S(1)}, s32[8]{0:T(128)}, u32[]{:S(2)}) copy-start(s32[8]{0:T(128)} %own_ref.1) | copy-start | bytes 100
  0.6 0.7 %copy-start.3 = (s32[6]{0:T(128)S(1)}, s32[6]{0:T(128)}, u32[]{:S(2)}) copy-start(s32[6]{0:T(128)} %seq_ref.1) | copy-start | bytes 76
  0.7 0.7 %copy-start.2 = (s32[128]{0:T(128)S(1)}, s32[128]{0:T(128)}, u32[]{:S(2)}) copy-start(s32[128]{0:T(128)} %param.7) | copy-start | bytes 1540
  1.3 1.1 %copy-start = (bf16[3,128,768]{2,1,0:T(8,128)(2,1)S(1)}, bf16[3,128,768]{2,1,0:T(8,128)(2,1)}, u32[]{:S(2)}) copy-start(bf16[3,128,768]{2,1,0:T(8,128)(2,1)} %w_ref.1) | copy-start | bytes 1769476
  2.4 1.1 %copy-start.1 = (bf16[3,128,768]{2,1,0:T(8,128)(2,1)S(1)}, bf16[3,128,768]{2,1,0:T(8,128)(2,1)}, u32[]{:S(2)}) copy-start(bf16[3,128,768]{2,1,0:T(8,128)(2,1)} %v_ref.1) | copy-start | bytes 1769476

commit v3 on v2

--- a/solution.py
+++ b/solution.py
@@ -61,7 +61,7 @@
     for j, t in ((0, other), (1, 1)):
         swaps.append(to(w_ref.at[t], wx.at[j], xs_sem.at[1 + 2 * j], xr_sem.at[1 + 2 * j], space=peer))
         swaps.append(to(v_ref.at[t], vx.at[j], xs_sem.at[2 + 2 * j], xr_sem.at[2 + 2 * j], space=peer))
-    for swap in swaps[:3]:
+    for swap in swaps:
         swap.start()
 
     def set_trig(q, row):
@@ -139,12 +139,13 @@
             tx[j][m, slot, k * block:(k + 1) * block, :] = value.astype(BF16)
         hop(j, m, slot, dst_slot, znext).start()
 
-    def reduce(j, m):
+    def reduce_end(j, m):
         @pl.when(is_end)
         def _():
             for i, far in enumerate((3, 2, 1)):
                 send(j, m, i, i, far, inner, None)
 
+    def reduce_mid(j, m):
         @pl.when(is_mid)
         def _():
             for i, far in enumerate((3, 2)):
@@ -185,10 +186,6 @@
     def store_g1(k, value):
         gfin1[...] = value
 
-    for swap in swaps[:3]:
-        swap.wait_send()
-    for swap in swaps[3:]:
-        swap.start()
     swaps[0].wait_recv()
     set_trig(1, phx[...])
     for j in range(2):
@@ -196,10 +193,11 @@
         swaps[2 + 2 * j].wait_recv()
         build(1, wx.at[j], vx.at[j])
         part[j, 0] += transposed_dot(left[...], right[0]) * scale_sites
-        reduce(j, 0)
+        reduce_end(j, 0)
+        reduce_mid(j, 0)
         part[j, 1] += transposed_dot(left[...], right[1]) * scale_sites
     for j in range(2):
-        reduce(j, 1)
+        reduce_end(j, 1)
 
     half = pl.ds(pl.multiple_of(x * block, 16), block)
     half_peer = pl.ds(pl.multiple_of((1 - x) * block, 16), block)
@@ -209,6 +207,7 @@
     give0.start()
     finish(1, 0, store_field1)
     give1.start()
+    reduce_mid(0, 1)
     give0.wait_recv()
     give1.wait_recv()
     sibling = to(
@@ -216,6 +215,7 @@
     )
     sibling.start()
     strips_ref[other] = fields[3 * c + other, half, :].astype(F32)
+    reduce_mid(1, 1)
     sibling.wait_recv()
 
     def weight(t, k):
@@ -264,7 +264,7 @@
     margin_ref[2:3, :n] = total[8:9]
     margin_ref[2:3, n:] = total[9:10]
 
-    for swap in swaps[3:]:
+    for swap in swaps:
         swap.wait_send()
     for j in range(2):
         for m in range(2):
@@ -333,7 +333,7 @@
             dma((nspace,)),
         ],
         compiler_params=pltpu.CompilerParams(
-            collective_id=0, has_side_effects=True, vmem_limit_bytes=48 * 1024 * 1024
+            collective_id=0, has_side_effects=True, vmem_limit_bytes=60 * 1024 * 1024
         ),
         cost_estimate=pl.CostEstimate(
             flops=16 * tdev * sdev * n * n, bytes_accessed=4 * tdev * sdev * width, transcendentals=0

time: 64.6 us -> 60.9 us (0.943)
  local copies, waits for them, and re-layouts: 4.15 us -> 2.41 us
  Pallas kernels: 59.1 us -> 57.7 us
    unnamed x12 -> x4, local copies, waits for them, and re-layouts: 4.15 us -> 2.41 us
    pallas_call x1, Pallas kernels: 59.1 us -> 57.7 us  [fused(): pl.pallas_call(functools.partial(kernel, tdev * ntm), out_shape=(jax.Shap...]
where the time goes in v3:
time: 60.9 us; the launch traced here: 60.7 us
  Pallas kernels  57.7 us (95%)
  local copies, waits for them, and re-layouts  2.41 us (4%)
  between operations  0.65 us (1%)
    pallas_call x1, Pallas kernels, fused(): pl.pallas_call(functools.partial(kernel, tdev * ntm), out_shape=(jax.Shap...  57.7 us
    unnamed x4, local copies, waits for them, and re-layouts  2.41 us

profile of v3, /device:TPU:0, one launch (start us, length us, event | category | flops | bytes accessed | tf_op | source)
XLA Modules:
  0.0 60.7 jit_solution(16916518169780735841)
XLA Ops:
  0.6 57.7 %shard_map.68 = (f32[3,48,768]{2,1,0:T(8,128)}, f32[3,768]{1,0:T(4,128)}) custom-call(bf16[3,128,768]{2,1,0:T(8,128)(2,1)} %w_ref.1, bf16[3,128,768]{2,1,0:T(8,128)(2,1)} %v_ref.1, s32[1,128]{1,0:T(1,128)} %bitcast.3, s32[6]{0:T(128)} %seq_ref.1, s32[8]{0:T(128)} %own_ref.1), custom_call_target="tpu_custom_call" | custom-call | flops 905969664 | bytes 1179648 | tf_op jit(solution)/shard_map/pallas_call | solution.py:290
  58.3 0.0 copy-start
  58.3 1.8 %copy.9 = f32[48,3,768]{2,0,1:T(8,128)} copy(f32[48,3,768]{2,0,1:T(8,128)} %bitcast.2) | data formatting | bytes 884736
  60.1 0.0 copy-done
  60.1 0.6 copy.10
Async XLA Ops:
  58.3 1.8 %copy-start = (f32[3,768]{1,0:T(4,128)S(1)}, f32[3,768]{1,0:T(4,128)}, u32[]{:S(2)}) copy-start(f32[3,768]{1,0:T(4,128)} %get-tuple-element.9) | copy-start | bytes 27652
